TPU v7x, 512 devices: a whole 4x4x16 slice. The times are simulated.
512 devices in a mesh: dp: 32 (over z_lo, y), mp: 16 (over x, z_hi, core).
Axes of the slice: x: 4, y: 4, z: 16 (z_hi: 2, z_lo: 8; z = z_hi * 8 + z_lo), core: 2. Of those that a mesh axis runs over, the one named last changes fastest.
Arguments:
- cotangent: bfloat16 [16384, 6144], P('dp', 'mp'), may hold values from -24 to 24
- out_weight: bfloat16 [4096, 6144], P('mp'), may hold values from -0.09375 to 0.09375
- query_raw: bfloat16 [16384, 4096], P('dp', 'mp'), may hold values from -200 to 200
- key_raw: bfloat16 [16384, 4096], P('dp', 'mp'), may hold values from -200 to 200
- value: bfloat16 [16384, 4096], P('dp', 'mp'), may hold values from -6 to 6
- query_gain: float32 [32, 128], P('mp'), may hold values from 0.5 to 5
- key_gain: float32 [32, 128], P('mp'), may hold values from 0.5 to 5
Outputs:
- query_grad: bfloat16 [16384, 4096], P('dp', 'mp')
- key_grad: bfloat16 [16384, 4096], P('dp', 'mp')
- value_gradient: bfloat16 [16384, 4096], P('dp', 'mp')
- out_weight_grad: bfloat16 [4096, 6144], P(('mp', 'dp'))
- query_gain_grad: float32 [32, 128], P('mp')
- key_gain_grad: float32 [32, 128], P('mp')
All inputs are finite; a program needn't handle non-finite values.
Results may differ from a plain program's by a relative error of at most 0.03.
The roundings to bfloat16 on the way count: a program that leaves them out, or rounds other values in their place, can miss the bound.
Values may be sent and summed in bfloat16 or wider, within the bound.
A program may use at most 64 MiB of HBM per device.

v0:
```python
import jax
import jax.numpy as jnp
from jax import lax
from jax.sharding import PartitionSpec as P

PATCHES = 256


EPSILON = 1e-06


def normalize(raw_values):
    floats = raw_values.astype(jnp.float32)
    center = floats - jnp.mean(floats, axis=-1, keepdims=True)
    inverse = lax.rsqrt(jnp.mean(center * center, axis=-1, keepdims=True) + EPSILON)
    return (center * inverse, inverse)


def norm_backward(upstream, normed, inverse, gain_row):
    scaled = upstream * gain_row
    centered = scaled - jnp.mean(scaled, axis=-1, keepdims=True)
    return inverse * (centered - normed * jnp.mean(scaled * normed, axis=-1, keepdims=True))


def local(cotangent, out_weight, query_raw, key_raw, value, query_gain, key_gain):
    groups = lax.axis_size("dp")
    tokens_here, local_width = query_raw.shape
    heads_here, head_dim = query_gain.shape
    images = tokens_here // PATCHES
    four_shape = (images, PATCHES, heads_here, head_dim)
    score_factor = head_dim ** (-0.5)
    contract_cols = (((1,), (1,)), ((), ()))
    contract_rows = (((0,), (0,)), ((), ()))
    query_norm, query_inverse = normalize(query_raw.reshape(four_shape))
    key_norm, key_inverse = normalize(key_raw.reshape(four_shape))
    query_applied = (query_norm * query_gain).astype(jnp.bfloat16)
    key_applied = (key_norm * key_gain).astype(jnp.bfloat16)
    attention_scores = (
        jnp.einsum(
            "iahd,ibhd->ihab", query_applied, key_applied, preferred_element_type=jnp.float32
        )
        * score_factor
    )
    probs = jax.nn.softmax(attention_scores, axis=-1)
    probability_reduced = probs.astype(jnp.bfloat16)
    value_four = value.reshape(four_shape)
    attended_values = (
        jnp.einsum(
            "ihab,ibhd->iahd", probability_reduced, value_four, preferred_element_type=jnp.float32
        )
        .astype(jnp.bfloat16)
        .reshape(tokens_here, local_width)
    )
    full_rows = lax.all_gather(cotangent, "mp", axis=1, tiled=True)
    attn_grad_full = lax.dot_general(
        full_rows, out_weight, contract_cols, preferred_element_type=jnp.float32
    )
    weight_sum = lax.psum_scatter(
        (
            lax.dot_general(
                attended_values, full_rows, contract_rows, preferred_element_type=jnp.float32
            )
            / groups
        ).astype(jnp.bfloat16),
        "dp",
        scatter_dimension=0,
        tiled=True,
    )
    grad_four = attn_grad_full.astype(jnp.bfloat16).reshape(four_shape)
    value_gradient = jnp.einsum(
        "ihab,iahd->ibhd", probability_reduced, grad_four, preferred_element_type=jnp.float32
    ).astype(jnp.bfloat16)
    probability_gradient = jnp.einsum(
        "iahd,ibhd->ihab", grad_four, value_four, preferred_element_type=jnp.float32
    )
    row_dot = jnp.sum(probs * probability_gradient, axis=-1, keepdims=True)
    score_gradient = (probs * (probability_gradient - row_dot) * score_factor).astype(jnp.bfloat16)
    query_applied_gradient = jnp.einsum(
        "ihab,ibhd->iahd", score_gradient, key_applied, preferred_element_type=jnp.float32
    )
    key_applied_gradient = jnp.einsum(
        "ihab,iahd->ibhd", score_gradient, query_applied, preferred_element_type=jnp.float32
    )
    gain_terms = (
        jnp.sum(query_applied_gradient * query_norm, axis=(0, 1)) / groups,
        jnp.sum(key_applied_gradient * key_norm, axis=(0, 1)) / groups,
    )
    query_gain_grad, key_gain_grad = lax.psum((gain_terms[0], gain_terms[1]), "dp")
    query_grad = norm_backward(query_applied_gradient, query_norm, query_inverse, query_gain)
    key_grad = norm_backward(key_applied_gradient, key_norm, key_inverse, key_gain)
    return (
        query_grad.astype(jnp.bfloat16).reshape(tokens_here, local_width),
        key_grad.astype(jnp.bfloat16).reshape(tokens_here, local_width),
        value_gradient.reshape(tokens_here, local_width),
        weight_sum,
        query_gain_grad,
        key_gain_grad,
    )


def solution(mesh):
    return jax.shard_map(
        local,
        mesh=mesh,
        in_specs=(
            P("dp", "mp"),
            P("mp", None),
            P("dp", "mp"),
            P("dp", "mp"),
            P("dp", "mp"),
            P("mp", None),
            P("mp", None),
        ),
        out_specs=(
            P("dp", "mp"),
            P("dp", "mp"),
            P("dp", "mp"),
            P(("mp", "dp"), None),
            P("mp", None),
            P("mp", None),
        ),
        check_vma=False,
    )
```

profile of v0, /device:TPU:2, one launch (start us, length us, event | category | flops | bytes accessed | tf_op | source)
XLA Modules:
  0.0 419.5 jit_solution(6647989591902293220)
XLA Ops:
  8.0 2.2 reshape.87
  10.2 2.1 copy.90
  12.2 1.7 reduce_sum.108
  13.9 2.0 reshape.88
  15.9 2.1 copy.92
  18.0 2.4 reduce_sum.110
  22.6 1.2 multiply_reduce_fusion.6
  25.0 2.2 multiply_convert_fusion.2
  27.1 2.5 fusion.30
  29.6 2.6 fusion.10
  32.3 1.2 copy.106
  33.5 132.0 %all-gather.2.cloned.1.call-done = bf16[512,6144]{1,0:T(8,128)(2,1)} async-done(((bf16[512,384]{1,0:T(8,128)(2,1)}), bf16[512,6144]{1,0:T(8,128)(2,1)}) %all-gather.2.cloned.1.call-update) | async-done | bytes 6291472 | tf_op jit(solution)/shard_map/all_gather | solution.py:54
  165.5 6.3 %fusion.2 = bf16[256,6144]{1,0:T(8,128)(2,1)} fusion(bf16[512,6144]{1,0:T(8,128)(2,1)} %all-gather.2.cloned.1.call-done, bf16[64,8,2,128]{3,2,1,0:T(2,128)(2,1)S(1)} %bitcast.41), kind=kOutput, calls=%fused_computation.3 | convolution fusion | flops 1613758464 | bytes 9699328 | tf_op jit(solution)/shard_map/dot_general | solution.py:60
  171.8 5.3 %convolution_convert_fusion = bf16[512,256]{1,0:T(8,128)(2,1)} fusion(bf16[512,6144]{1,0:T(8,128)(2,1)} %all-gather.2.cloned.1.call-done, bf16[256,6144]{1,0:T(8,128)(2,1)S(1)} %copy-done), kind=kOutput, calls=%fused_computation.13 | convolution fusion | flops 1610743808 | bytes 9699328 | tf_op jit(solution)/shard_map/dot_general | solution.py:55
  179.0 2.3 fusion.22
  181.3 3.7 multiply_reduce_fusion.2
  185.1 2.1 multiply_convert_fusion.1
  187.1 1.1 copy.98
  189.0 3.8 multiply_reduce_fusion.1
  192.8 2.1 multiply_convert_fusion
  196.7 2.6 fusion.9
  199.3 1.1 copy.103
  201.1 116.9 %all-reduce = (f32[2,128]{1,0:T(2,128)}, f32[2,128]{1,0:T(2,128)}) all-reduce(f32[2,128]{1,0:T(2,128)S(1)} %broadcast_multiply_fusion.7, f32[2,128]{1,0:T(2,128)S(1)} %broadcast_multiply_fusion.6), channel_id=1, replica_groups=mesh['dp'=32,'mp'=16] {'dp'}, use_global_device_ids=true, to_apply=%region_13.0 | all-reduce | flops 512 | bytes 4096 | tf_op jit(solution)/shard_map/psum | solution.py:88
  318.0 94.6 %reduce-scatter.2.cloned.1.call-done = bf16[8,6144]{1,0:T(8,128)(2,1)} async-done(((bf16[256,6144]{1,0:T(8,128)(2,1)}), bf16[8,6144]{1,0:T(8,128)(2,1)}) %reduce-scatter.2.cloned.1.call-update) | async-done | bytes 98320 | tf_op jit(solution)/shard_map/reduce_scatter | solution.py:58
  (32 shorter events, 9.4 us)
Async XLA Ops:
  7.2 164.7 %copy-start = (bf16[256,6144]{1,0:T(8,128)(2,1)S(1)}, bf16[256,6144]{1,0:T(8,128)(2,1)}, u32[]{:S(2)}) copy-start(bf16[256,6144]{1,0:T(8,128)(2,1)} %param.8) | copy-start | bytes 9437188
  7.2 17.8 %copy-start.2 = (f32[2,128]{1,0:T(2,128)S(1)}, f32[2,128]{1,0:T(2,128)}, u32[]{:S(2)}) copy-start(f32[2,128]{1,0:T(2,128)} %param.12) | copy-start | bytes 3076
  7.2 17.8 %copy-start.3 = (f32[2,128]{1,0:T(2,128)S(1)}, f32[2,128]{1,0:T(2,128)}, u32[]{:S(2)}) copy-start(f32[2,128]{1,0:T(2,128)} %param.13) | copy-start | bytes 3076
  7.2 158.3 %all-gather.2.cloned.1.call-start = ((), (), s32[]{:S(2)}) async-start(), calls=%async_computation.1 | async-start | bytes 6684672 | tf_op jit(solution)/shard_map/all_gather | solution.py:54
  7.9 404.7 %reduce-scatter.2.cloned.1.call-start = ((), (), s32[]{:S(2)}) async-start(), calls=%async_computation.2 | async-start | bytes 3244032 | tf_op jit(solution)/shard_map/reduce_scatter | solution.py:58
  22.6 7.1 %copy-start.1 = (bf16[2,256,2,128]{3,2,1,0:T(2,128)(2,1)}, bf16[2,256,2,128]{3,2,1,0:T(2,128)(2,1)S(1)}, u32[]{:S(2)}) copy-start(bf16[2,256,2,128]{3,2,1,0:T(2,128)(2,1)S(1)} %reshape.82) | copy-start | bytes 786436
Sparse Core Ops, SparseCore 0:
  11.2 154.2 all-gather.1
  171.9 240.6 reduce-scatter.1
where the time goes:
time: 420 us; the launch traced here: 419 us
  waiting for transfers between devices  227 us (54%)
  blocking collectives  117 us (28%)
  matrix products  29.1 us (7%)
  local copies, waits for them, and re-layouts  19.2 us (5%)
  between operations  14.2 us (3%)
  other arithmetic  12.7 us (3%)
    all_gather x1, waiting for transfers between devices, local(): full_rows = lax.all_gather(cotangent, 'mp', axis=1, tiled=True)  132 us
    psum x1, blocking collectives, local(): lax.psum((gain_terms[0], gain_terms[1]), 'dp')  117 us
    reduce_scatter x1, waiting for transfers between devices, local(): lax.psum_scatter((lax.dot_general(attended_values, full_rows, contract_ro...  94.6 us
  transfers between devices with their start and end apart: 2, of which 2 were waited for; matrix products, arithmetic and copies ran while one was open for 13% of the time, Pallas kernels for 0%

commit v1 on v0

v1 whole, which is shorter than its diff:
```python
import jax
import jax.numpy as jnp
from jax import lax
from jax.experimental import pallas as pl
from jax.experimental.pallas import tpu as pltpu
from jax.sharding import PartitionSpec as P

MESH = pl.DeviceIdType.MESH
F32 = jnp.float32
BF16 = jnp.bfloat16

PATCHES = 256
HEAD = 128
EPSILON = 1e-06
TOK = 512
LANES = 128
CHIPS = 8
BLOCKS = 3
UNITS = CHIPS * BLOCKS
HALF = UNITS // 2
GROUP = 6
AHEAD = 2
BEHIND = 3
NY = 4
NZ = 8
ROWS = 16

NT = (((1,), (1,)), ((), ()))
TN = (((0,), (0,)), ((), ()))


def dot(a, b, dims=(((1,), (0,)), ((), ()))):
    return lax.dot_general(a, b, dims, preferred_element_type=F32)


def normalize(raw):
    floats = raw.astype(F32)
    center = floats - jnp.mean(floats, axis=-1, keepdims=True)
    inverse = lax.rsqrt(jnp.mean(center * center, axis=-1, keepdims=True) + EPSILON)
    return center * inverse, inverse


def norm_backward(upstream, normed, inverse, gain):
    scaled = upstream * gain
    centered = scaled - jnp.mean(scaled, axis=-1, keepdims=True)
    return inverse * (centered - normed * jnp.mean(scaled * normed, axis=-1, keepdims=True))


def kernel(
    cot_hbm, w_hbm, q_hbm, k_hbm, v_hbm, qg_ref, kg_ref,
    qgrad_ref, kgrad_ref, vgrad_ref, wgrad_ref, qgg_ref, kgg_ref,
    ag, w, qraw, kraw, v, qn, kn, qinv, kinv, qu, ku, probs, att, acc,
    ysend, yrecv, zsend, zrecv, gown, gy, gsum, gz,
    local_sem, send_sem, x_sem, core_sem, y_sem, z_sem, g_sem,
):
    d = lax.axis_index("dp")
    m = lax.axis_index("mp")
    y = lax.rem(d, NY)
    zl = d // NY
    x = m // 4
    zh = lax.rem(m // 2, 2)
    c = lax.rem(m, 2)

    def x_peer(k):
        return (d, lax.rem(x + k, 4) * 4 + zh * 2 + c)

    def y_peer(k):
        return (zl * NY + lax.rem(y + k, NY), m)

    def z_peer(k):
        return (lax.rem(zl + k, NZ) * NY + y, m)

    core_peer = (d, m + 1 - 2 * c)
    far_peer = (d, x * 4 + (1 - zh) * 2 + c)

    barrier = pltpu.get_barrier_semaphore()
    peers = [far_peer, core_peer]
    peers += [x_peer(k) for k in (1, 2, 3)]
    peers += [y_peer(k) for k in (1, 2, 3)]
    peers += [z_peer(k) for k in range(1, NZ)]
    for peer in peers:
        pl.semaphore_signal(barrier, inc=1, device_id=peer, device_id_type=MESH)

    loads = [
        pltpu.make_async_copy(q_hbm, qraw, local_sem.at[0]),
        pltpu.make_async_copy(k_hbm, kraw, local_sem.at[1]),
        pltpu.make_async_copy(v_hbm, v, local_sem.at[2]),
    ]
    for j in range(BLOCKS):
        loads.append(
            pltpu.make_async_copy(
                cot_hbm.at[:, pl.ds(j * LANES, LANES)], ag.at[0, j, c], local_sem.at[3 + j]
            )
        )
    loads.append(pltpu.make_async_copy(w_hbm, w, local_sem.at[3 + BLOCKS]))
    for load in loads:
        load.start()
    for load in loads[:3]:
        load.wait()

    factor = HEAD ** (-0.5)
    acc[...] = jnp.zeros_like(acc)

    for image in range(2):
        for head in range(2):
            pair = image * 2 + head
            rows = pl.ds(image * PATCHES, PATCHES)
            cols = pl.ds(head * HEAD, HEAD)
            normed, inverse = normalize(qraw[rows, cols])
            qn[pair] = normed
            qinv[pair] = inverse
            query = (normed * qg_ref[pl.ds(head, 1), :]).astype(BF16)
            qu[pair] = query
            normed, inverse = normalize(kraw[rows, cols])
            kn[pair] = normed
            kinv[pair] = inverse
            keys = (normed * kg_ref[pl.ds(head, 1), :]).astype(BF16)
            ku[pair] = keys
            scores = dot(keys, query, NT) * factor
            weights = jnp.exp(scores - jnp.max(scores, axis=0, keepdims=True))
            weights = weights / jnp.sum(weights, axis=0, keepdims=True)
            probs[pair] = weights
            attended = dot(v[rows, cols], weights.astype(BF16), TN)
            att[cols, rows] = attended.astype(BF16)

    for load in loads[3:]:
        load.wait()
    pl.semaphore_wait(barrier, len(peers))

    def remote(src, dst, sent, landed, peer):
        return pltpu.make_async_remote_copy(
            src_ref=src, dst_ref=dst, send_sem=sent, recv_sem=landed,
            device_id=peer, device_id_type=MESH,
        )

    def send_x(slot, j):
        for k in (1, 3, 2):
            remote(
                ag.at[slot, j, c], ag.at[slot + 4 - k, j, c],
                send_sem.at[1], x_sem.at[slot + 4 - k, j], x_peer(k),
            ).start()

    def send_core(slot, j):
        remote(
            ag.at[slot, j, c], ag.at[slot, j, c],
            send_sem.at[2], core_sem.at[slot, j], core_peer,
        ).start()

    for j in range(BLOCKS):
        remote(ag.at[0, j, c], ag.at[4, j, c], send_sem.at[0], x_sem.at[4, j], far_peer).start()
        send_core(0, j)
        send_x(0, j)

    def place(unit):
        half = unit // HALF
        rest = lax.rem(unit, HALF)
        return half, rest // 4, half * 4 + lax.rem(rest, 4)

    def await_block(slot, j, sem):
        pltpu.make_async_copy(ag.at[slot, j, 0], ag.at[slot, j, 0], sem).wait()

    def forward(unit):
        half, j, slot = place(unit)

        @pl.when(slot != 0)
        def _():
            await_block(slot, j, x_sem.at[slot, j])

            @pl.when(slot == 4)
            def _():
                send_x(4, j)

            send_core(slot, j)

    def column(unit):
        half, j, slot = place(unit)
        owner = lax.rem(x + lax.rem(slot, 4), 4) * 2 + lax.rem(zh + half, 2)
        return pl.multiple_of(owner * 768 + j * LANES, LANES)

    def project(unit):
        half, j, slot = place(unit)
        await_block(slot, j, core_sem.at[slot, j])
        start = column(unit)
        weight = jnp.concatenate(
            [w[:, pl.ds(start, LANES)], w[:, pl.ds(start + 384, LANES)]], axis=1
        )
        for part in range(2):
            rows = pl.ds(part * 256, 256)
            block = jnp.concatenate([ag[slot, j, 0, rows, :], ag[slot, j, 1, rows, :]], axis=1)
            acc[rows, :] += dot(block, weight, NT)
        block = jnp.concatenate([ag[slot, j, 0], ag[slot, j, 1]], axis=1)
        terms = dot(att[...], block) * (1.0 / 32.0)
        first = terms[:, :LANES].reshape(NZ, NY, 8, LANES)
        second = terms[:, LANES:].reshape(NZ, NY, 8, LANES)
        both = jnp.concatenate([first, second], axis=2).astype(BF16)
        for part in range(NY):
            ysend[unit, part] = both[:, part]
        for k in (1, 3, 2):
            remote(
                ysend.at[unit, lax.rem(y + k, NY)], yrecv.at[unit, k - 1],
                send_sem.at[3], y_sem.at[unit], y_peer(k),
            ).start()

    def sum_y(unit):
        pltpu.make_async_copy(yrecv.at[unit], yrecv.at[unit], y_sem.at[unit]).wait()
        total = ysend[unit, y].astype(F32)
        for k in range(3):
            total += yrecv[unit, k].astype(F32)
        zsend[:, unit] = total.astype(BF16)

    def send_z(group):
        span = pl.ds(group * GROUP, GROUP)
        for k in range(1, NZ):
            remote(
                zsend.at[lax.rem(zl + k, NZ), span], zrecv.at[zl, span],
                send_sem.at[4], z_sem.at[group], z_peer(k),
            ).start()

    for unit in range(AHEAD):
        forward(jnp.int32(unit))

    @pl.loop(0, UNITS)
    def _(unit):
        @pl.when(unit + AHEAD < UNITS)
        def _():
            forward(unit + AHEAD)

        project(unit)

        @pl.when(unit >= BEHIND)
        def _():
            sum_y(unit - BEHIND)

            @pl.when(lax.rem(unit - BEHIND, GROUP) == GROUP - 1)
            def _():
                send_z((unit - BEHIND) // GROUP)

    gains = [[None, None], [None, None]]

    def backward(image, head):
        pair = image * 2 + head
        rows = pl.ds(image * PATCHES, PATCHES)
        cols = pl.ds(head * HEAD, HEAD)
        grad = acc[rows, cols].astype(BF16)
        weights = probs[pair]
        vgrad_ref[rows, cols] = dot(weights.astype(BF16), grad).astype(BF16)
        upstream = dot(v[rows, cols], grad, NT)
        row_dot = jnp.sum(weights * upstream, axis=0, keepdims=True)
        score = (weights * (upstream - row_dot) * factor).astype(BF16)
        kup = dot(score, qu[pair])
        qup = dot(score, ku[pair], TN)
        for which, (up, normed, inverse, gain, out) in enumerate((
            (qup, qn[pair], qinv[pair], qg_ref[pl.ds(head, 1), :], qgrad_ref),
            (kup, kn[pair], kinv[pair], kg_ref[pl.ds(head, 1), :], kgrad_ref),
        )):
            part = jnp.sum(up * normed, axis=0, keepdims=True)
            old = gains[which][head]
            gains[which][head] = part if old is None else old + part
            out[rows, cols] = norm_backward(up, normed, inverse, gain).astype(BF16)

    backward(0, 0)
    backward(0, 1)
    for unit in range(UNITS - BEHIND, UNITS):
        sum_y(unit)
    send_z(UNITS // GROUP - 1)
    backward(1, 0)
    backward(1, 1)

    gown[...] = jnp.zeros_like(gown)
    for which in range(2):
        for head in range(2):
            gown[pl.ds(which * 2 + head, 1), :] = gains[which][head] * (1.0 / 32.0)
    for k in (1, 2, 3):
        remote(gown, gy.at[k - 1], send_sem.at[5], g_sem.at[0], y_peer(k)).start()
    pltpu.make_async_copy(gy, gy, g_sem.at[0]).wait()
    gsum[...] = gown[...] + gy[0] + gy[1] + gy[2]
    for k in range(1, NZ):
        remote(gsum, gz.at[k - 1], send_sem.at[6], g_sem.at[1], z_peer(k)).start()

    zrecv[zl] = zsend[zl]
    for group in range(UNITS // GROUP):
        span = pl.ds(group * GROUP, GROUP)
        landed = zrecv.at[pl.ds(0, NZ - 1), span]
        pltpu.make_async_copy(landed, landed, z_sem.at[group]).wait()

    @pl.loop(0, UNITS)
    def _(unit):
        total = zrecv[0, unit].astype(F32)
        for k in range(1, NZ):
            total += zrecv[k, unit].astype(F32)
        total = total.astype(BF16)
        start = column(unit)
        wgrad_ref[:, pl.ds(start, LANES)] = total[:8]
        wgrad_ref[:, pl.ds(start + 384, LANES)] = total[8:]

    pltpu.make_async_copy(gz, gz, g_sem.at[1]).wait()
    total = gsum[...]
    for k in range(NZ - 1):
        total += gz[k]
    qgg_ref[...] = total[0:2]
    kgg_ref[...] = total[2:4]

    pltpu.make_async_copy(ag.at[0, :, 0], ag.at[0, :, 0], send_sem.at[0]).wait()
    pltpu.make_async_copy(ag.at[pl.ds(0, 3)], ag.at[pl.ds(0, 3)], send_sem.at[1]).wait()
    pltpu.make_async_copy(ag.at[pl.ds(0, 4)], ag.at[pl.ds(0, 4)], send_sem.at[2]).wait()
    pltpu.make_async_copy(yrecv, yrecv, send_sem.at[3]).wait()
    sent = zrecv.at[pl.ds(0, NZ - 1)]
    pltpu.make_async_copy(sent, sent, send_sem.at[4]).wait()
    pltpu.make_async_copy(gy, gy, send_sem.at[5]).wait()
    pltpu.make_async_copy(gz, gz, send_sem.at[6]).wait()


def local(cotangent, out_weight, query_raw, key_raw, value, query_gain, key_gain):
    anywhere = pl.BlockSpec(memory_space=pl.ANY)
    vmem = pl.BlockSpec(memory_space=pltpu.VMEM)
    pair = (4, PATCHES, HEAD)
    outs = pl.pallas_call(
        kernel,
        out_shape=(
            jax.ShapeDtypeStruct((TOK, 256), BF16),
            jax.ShapeDtypeStruct((TOK, 256), BF16),
            jax.ShapeDtypeStruct((TOK, 256), BF16),
            jax.ShapeDtypeStruct((8, 6144), BF16),
            jax.ShapeDtypeStruct((2, HEAD), F32),
            jax.ShapeDtypeStruct((2, HEAD), F32),
        ),
        in_specs=[anywhere] * 5 + [vmem] * 2,
        out_specs=[vmem] * 6,
        scratch_shapes=[
            pltpu.VMEM((CHIPS, BLOCKS, 2, TOK, LANES), BF16),
            pltpu.VMEM((256, 6144), BF16),
            pltpu.VMEM((TOK, 256), BF16),
            pltpu.VMEM((TOK, 256), BF16),
            pltpu.VMEM((TOK, 256), BF16),
            pltpu.VMEM(pair, F32),
            pltpu.VMEM(pair, F32),
            pltpu.VMEM((4, PATCHES, 1), F32),
            pltpu.VMEM((4, PATCHES, 1), F32),
            pltpu.VMEM(pair, BF16),
            pltpu.VMEM(pair, BF16),
            pltpu.VMEM((4, PATCHES, PATCHES), F32),
            pltpu.VMEM((256, TOK), BF16),
            pltpu.VMEM((TOK, 256), F32),
            pltpu.VMEM((UNITS, NY, NZ, ROWS, LANES), BF16),
            pltpu.VMEM((UNITS, NY - 1, NZ, ROWS, LANES), BF16),
            pltpu.VMEM((NZ, UNITS, ROWS, LANES), BF16),
            pltpu.VMEM((NZ, UNITS, ROWS, LANES), BF16),
            pltpu.VMEM((8, LANES), F32),
            pltpu.VMEM((NY - 1, 8, LANES), F32),
            pltpu.VMEM((8, LANES), F32),
            pltpu.VMEM((NZ - 1, 8, LANES), F32),
            pltpu.SemaphoreType.DMA((4 + BLOCKS,)),
            pltpu.SemaphoreType.DMA((7,)),
            pltpu.SemaphoreType.DMA((CHIPS, BLOCKS)),
            pltpu.SemaphoreType.DMA((CHIPS, BLOCKS)),
            pltpu.SemaphoreType.DMA((UNITS,)),
            pltpu.SemaphoreType.DMA((UNITS // GROUP,)),
            pltpu.SemaphoreType.DMA((2,)),
        ],
        compiler_params=pltpu.CompilerParams(
            collective_id=0, has_side_effects=True, vmem_limit_bytes=48 << 20
        ),
        cost_estimate=pl.CostEstimate(
            flops=4 * 10**9, bytes_accessed=6 * 10**6, transcendentals=4 * 65536
        ),
        name="attention_backward",
    )(cotangent, out_weight, query_raw, key_raw, value, query_gain, key_gain)
    return tuple(outs)


def solution(mesh):
    return jax.shard_map(
        local,
        mesh=mesh,
        in_specs=(
            P("dp", "mp"),
            P("mp", None),
            P("dp", "mp"),
            P("dp", "mp"),
            P("dp", "mp"),
            P("mp", None),
            P("mp", None),
        ),
        out_specs=(
            P("dp", "mp"),
            P("dp", "mp"),
            P("dp", "mp"),
            P(("mp", "dp"), None),
            P("mp", None),
            P("mp", None),
        ),
        check_vma=False,
    )
```

time: 420 us -> 101 us (0.24)
  the two profiles are of different devices: /device:TPU:2 before, /device:TPU:1 now
where the time goes in v1:
time: 101 us; the launch traced here: 99.4 us
  Pallas kernels  87.8 us (87%)
  local copies, waits for them, and re-layouts  11 us (11%)
    pallas_call x1, Pallas kernels, local(): pl.pallas_call(kernel, out_shape=(jax.ShapeDtypeStruct((TOK, 256), BF16),...  87.8 us
    unnamed x20, local copies, waits for them, and re-layouts  11 us

profile of v1, /device:TPU:1, one launch (start us, length us, event | category | flops | bytes accessed | tf_op | source)
XLA Modules:
  0.0 99.4 jit_solution(3231093558489357525)
XLA Ops:
  0.6 0.0 copy-start
  0.6 1.9 %copy-done = bf16[256,6144]{1,0:T(8,128)(2,1)S(1)} copy-done((bf16[256,6144]{1,0:T(8,128)(2,1)S(1)}, bf16[256,6144]{1,0:T(8,128)(2,1)}, u32[]{:S(2)}) %copy-start) | copy-done | bytes 3145752
  2.5 0.0 copy-start.1
  2.5 1.0 copy-done.1
  3.5 0.0 copy-start.2
  3.5 0.9 copy-done.2
  4.5 0.0 copy-start.3
  4.5 0.9 copy-done.3
  5.4 0.0 copy-start.4
  5.4 0.9 copy-done.4
  6.4 0.0 copy-start.5
  6.4 0.7 copy-done.5
  7.1 0.0 copy-start.6
  7.1 0.7 copy-done.6
  7.7 87.8 %attention_backward.1 = (bf16[512,256]{1,0:T(8,128)(2,1)S(1)}, bf16[512,256]{1,0:T(8,128)(2,1)S(1)}, bf16[512,256]{1,0:T(8,128)(2,1)S(1)}, bf16[8,6144]{1,0:T(8,...) custom-call(bf16[512,384]{1,0:T(8,128)(2,1)S(1)} %copy-done.1, bf16[256,6144]{1,0:T(8,128)(2,1)S(1)} %copy-done, ...), custom_call_target="tpu_custom_call" | custom-call | flops 4000000000 | bytes 6000000 | tf_op jit(solution)/shard_map/attention_backward/pallas_call | solution.py:317
  95.6 0.7 copy.19
  96.3 0.7 copy.20
  97.0 0.7 copy.21
  97.7 0.6 copy.22
  98.3 0.6 copy.23
  98.9 0.6 copy.24
Async XLA Ops:
  0.6 1.9 %copy-start = (bf16[256,6144]{1,0:T(8,128)(2,1)S(1)}, bf16[256,6144]{1,0:T(8,128)(2,1)}, u32[]{:S(2)}) copy-start(bf16[256,6144]{1,0:T(8,128)(2,1)} %w_hbm.1) | copy-start | bytes 9437188
  2.5 1.0 %copy-start.1 = (bf16[512,384]{1,0:T(8,128)(2,1)S(1)}, bf16[512,384]{1,0:T(8,128)(2,1)}, u32[]{:S(2)}) copy-start(bf16[512,384]{1,0:T(8,128)(2,1)} %cot_hbm.1) | copy-start | bytes 1179652
  3.5 0.9 copy-start.2
  4.5 0.9 copy-start.3
  5.4 0.9 copy-start.4
  6.4 0.7 copy-start.5
  7.1 0.7 copy-start.6

commit v2 on v1

v2 whole, which is shorter than its diff:
```python
import jax
import jax.numpy as jnp
from jax import lax
from jax.experimental import pallas as pl
from jax.experimental.pallas import tpu as pltpu
from jax.sharding import PartitionSpec as P

MESH = pl.DeviceIdType.MESH
F32 = jnp.float32
BF16 = jnp.bfloat16

PATCHES = 256
HEAD = 128
EPSILON = 1e-06
TOK = 512
LANES = 128
CHIPS = 8
BLOCKS = 3
UNITS = CHIPS * BLOCKS // 2
GROUP = 2
GROUPS = UNITS // GROUP
NY = 4
NZ = 8
ROWS = 16
REVERSED = (0, 4, 2, 6, 1, 5, 3, 7)

NT = (((1,), (1,)), ((), ()))
TN = (((0,), (0,)), ((), ()))


def dot(a, b, dims=(((1,), (0,)), ((), ()))):
    return lax.dot_general(a, b, dims, preferred_element_type=F32)


def normalize(raw):
    floats = raw.astype(F32)
    center = floats - jnp.mean(floats, axis=-1, keepdims=True)
    inverse = lax.rsqrt(jnp.mean(center * center, axis=-1, keepdims=True) + EPSILON)
    return center * inverse, inverse


def norm_backward(upstream, normed, inverse, gain):
    scaled = upstream * gain
    centered = scaled - jnp.mean(scaled, axis=-1, keepdims=True)
    return inverse * (centered - normed * jnp.mean(scaled * normed, axis=-1, keepdims=True))


def kernel(
    cot_hbm, w_hbm, q_hbm, k_hbm, v_hbm, qg_ref, kg_ref,
    qgrad_ref, kgrad_ref, vgrad_ref, wgrad_ref, qgg_ref, kgg_ref,
    ag, transit, w2, qraw, kraw, v, qn, kn, qinv, kinv, qu, ku, probs, att, acc, accr,
    ysend, yrecv, z0, r0, z1, r1, z2, r2, wsend, wrecv, gown, gy, gsum, gz,
    local_sem, send_sem, leg_sem, far_sem, x_sem, core_sem, acc_sem, out_sem, y1_sem, y_sem, z_sem, gy_sem, gz_sem,
):
    d = lax.axis_index("dp")
    m = lax.axis_index("mp")
    y = lax.rem(d, NY)
    zl = d // NY
    x = m // 4
    zh = lax.rem(m // 2, 2)
    c = lax.rem(m, 2)
    z = zh * NZ + zl
    bits = [lax.rem(zl // step, 2) for step in (1, 2, 4)]

    def x_peer(k):
        return (d, lax.rem(x + k, 4) * 4 + zh * 2 + c)

    def y_peer(k):
        return (zl * NY + lax.rem(y + k, NY), m)

    def z_peer(k):
        other = lax.rem(z + k, 2 * NZ)
        return (lax.rem(other, NZ) * NY + y, x * 4 + (other // NZ) * 2 + c)

    def half_peer(stage):
        step = 1 << stage
        return ((zl + step - 2 * step * bits[stage]) * NY + y, m)

    core_peer = (d, m + 1 - 2 * c)

    barrier = pltpu.get_barrier_semaphore()
    peers = [z_peer(4), z_peer(12), core_peer, half_peer(0), half_peer(1)]
    peers += [x_peer(k) for k in (1, 3)]
    peers += [y_peer(k) for k in (1, 2, 3)]
    for peer in peers:
        pl.semaphore_signal(barrier, inc=1, device_id=peer, device_id_type=MESH)

    loads = [
        pltpu.make_async_copy(q_hbm, qraw, local_sem.at[0]),
        pltpu.make_async_copy(k_hbm, kraw, local_sem.at[1]),
        pltpu.make_async_copy(v_hbm, v, local_sem.at[2]),
    ]
    for j in range(BLOCKS):
        loads.append(
            pltpu.make_async_copy(
                cot_hbm.at[:, pl.ds(j * LANES, LANES)], ag.at[0, j], local_sem.at[3 + j]
            )
        )
    for chip in range(CHIPS):
        start = pl.multiple_of(chip * 768 + c * 384, LANES)
        loads.append(
            pltpu.make_async_copy(
                w_hbm.at[:, pl.ds(start, 384)], w2.at[c, chip], local_sem.at[3 + BLOCKS]
            )
        )
    for load in loads:
        load.start()

    def remote(src, dst, sent, landed, peer):
        return pltpu.make_async_remote_copy(
            src_ref=src, dst_ref=dst, send_sem=sent, recv_sem=landed,
            device_id=peer, device_id_type=MESH,
        )

    def landed(ref, sem):
        pltpu.make_async_copy(ref, ref, sem).wait()

    def send_x(slot, j):
        for k in (1, 3):
            remote(
                ag.at[slot, j], ag.at[slot + 4 - k, j],
                send_sem.at[1], x_sem.at[slot + 4 - k, j], x_peer(k),
            ).start()

    def part(p):
        return pl.ds(p * 256, 256)

    factor = HEAD ** (-0.5)

    def forward(image, head):
        pair = image * 2 + head
        rows = pl.ds(image * PATCHES, PATCHES)
        cols = pl.ds(head * HEAD, HEAD)
        normed, inverse = normalize(qraw[rows, cols])
        qn[pair] = normed
        qinv[pair] = inverse
        query = (normed * qg_ref[pl.ds(head, 1), :]).astype(BF16)
        qu[pair] = query
        normed, inverse = normalize(kraw[rows, cols])
        kn[pair] = normed
        kinv[pair] = inverse
        keys = (normed * kg_ref[pl.ds(head, 1), :]).astype(BF16)
        ku[pair] = keys
        scores = dot(keys, query, NT) * factor
        weights = jnp.exp(scores - jnp.max(scores, axis=0, keepdims=True))
        weights = weights / jnp.sum(weights, axis=0, keepdims=True)
        probs[pair] = weights
        attended = dot(v[rows, cols], weights.astype(BF16), TN)
        att[c, cols, rows] = attended.astype(BF16)

    for load in loads[:3]:
        load.wait()
    forward(0, 0)
    forward(0, 1)
    for load in loads[3:3 + BLOCKS]:
        load.wait()
    pl.semaphore_wait(barrier, len(peers))
    def send_leg(j):
        for p in range(2):
            remote(
                ag.at[0, j, part(p)], transit.at[j, p],
                send_sem.at[0], leg_sem.at[j, p], z_peer(4 + 8 * p),
            ).start()

    send_leg(0)
    send_leg(1)
    for j in range(BLOCKS):
        send_x(0, j)
    for chip in range(CHIPS):
        start = pl.multiple_of(chip * 768 + (1 - c) * 384, LANES)
        remote(
            w_hbm.at[:, pl.ds(start, 384)], w2.at[c, chip],
            send_sem.at[2], core_sem.at[0], core_peer,
        ).start()
    forward(1, 0)
    forward(1, 1)
    remote(att.at[c], att.at[c], send_sem.at[11], core_sem.at[1], core_peer).start()
    acc[...] = jnp.zeros_like(acc)
    landed(w2.at[c], local_sem.at[3 + BLOCKS])

    def arrive_weights():
        landed(w2.at[1 - c], core_sem.at[0])
        landed(att.at[1 - c], core_sem.at[1])

    def pass_on(j):
        for p in range(2):
            landed(transit.at[j, p], leg_sem.at[j, p])
            remote(
                transit.at[j, p], ag.at[4, j, part(p)],
                send_sem.at[0], far_sem.at[j, p], z_peer(4 + 8 * p),
            ).start()
        if j == 0:
            send_leg(2)

    def arrive_far(j):
        for p in range(2):
            landed(ag.at[4, j, part(p)], far_sem.at[j, p])
        send_x(4, j)

    def arrive_near(group):
        half, j = divmod(group, BLOCKS)
        for k, p in ((1, 1), (3, 0)):
            slot = half * 4 + k
            landed(ag.at[slot, j], x_sem.at[slot, j])
            remote(
                ag.at[slot, j, part(p)], ag.at[half * 4 + 2, j, part(p)],
                send_sem.at[1], x_sem.at[half * 4 + 2, j], x_peer(4 - k),
            ).start()

    def arrive_opposite(group):
        slot = (group // BLOCKS) * 4 + 2
        j = lax.rem(group, BLOCKS)
        landed(ag.at[slot, j], x_sem.at[slot, j])

    def place(unit):
        group = unit // GROUP
        half = group // BLOCKS
        near = 1 - lax.rem(unit, GROUP)
        owners = [
            lax.rem(x + near + k, 4) * 2 + lax.rem(zh + half, 2) for k in (0, 2)
        ]
        return half * 4 + near, owners, lax.rem(group, BLOCKS)

    def column(owner, core, j):
        return pl.multiple_of(owner * 768 + core * 384 + j * LANES, LANES)

    up, across, down = [lax.rem(y + k, NY) for k in (1, 2, 3)]

    def quads(p):
        return pl.ds(p * 4, 4)

    def send_y(unit, to, p, slot, sem, k):
        remote(
            ysend.at[unit, to, quads(p)], yrecv.at[unit, slot, quads(p)],
            send_sem.at[3], sem.at[unit], y_peer(k),
        ).start()

    def project(unit):
        slot, owners, j = place(unit)
        cols = pl.ds(pl.multiple_of(j * LANES, LANES), LANES)
        block = jnp.concatenate([ag[slot, j], ag[slot + 2, j]], axis=1)
        terms = [
            (dot(att[core], block) * (1.0 / 32.0)).reshape(NZ, NY, 8, 2 * LANES)
            for core in range(2)
        ]
        both = jnp.concatenate(terms, axis=2).astype(BF16)
        for to in range(NZ):
            for p in range(NY):
                for k in range(2):
                    ysend[unit, p, REVERSED[to], k] = both[to, p, :, k * LANES:(k + 1) * LANES]
        send_y(unit, across, 0, 0, y1_sem, 1)
        send_y(unit, across, 1, 0, y1_sem, 3)
        send_y(unit, up, 1, 1, y_sem, 1)
        send_y(unit, down, 0, 2, y_sem, 3)
        for core in range(2):
            weight = jnp.concatenate([w2[core, owner, :, cols] for owner in owners], axis=1)
            for p in range(2):
                block = jnp.concatenate([ag[slot, j, part(p)], ag[slot + 2, j, part(p)]], axis=1)
                acc[core, part(p), :] += dot(block, weight, NT)

    def span(group):
        return pl.ds(group * GROUP, GROUP)

    def stage_mid(group):
        @pl.loop(group * GROUP, group * GROUP + GROUP)
        def _(unit):
            landed(yrecv.at[unit, 0], y1_sem.at[unit])
            for to, p, slot, k in ((up, 0, 1, 1), (down, 1, 2, 3)):
                total = ysend[unit, to, quads(p)].astype(F32)
                total += yrecv[unit, 0, quads(p)].astype(F32)
                ysend[unit, to, quads(p)] = total.astype(BF16)
                send_y(unit, to, p, slot, y_sem, k)

    def stage_y(group):
        @pl.loop(group * GROUP, group * GROUP + GROUP)
        def _(unit):
            landed(yrecv.at[unit, pl.ds(1, 2)], y_sem.at[unit])
            total = ysend[unit, y].astype(F32)
            for k in (1, 2):
                total += yrecv[unit, k].astype(F32)
            z0[:, unit] = total.astype(BF16)

        remote(
            z0.at[pl.ds(4 - 4 * bits[0], 4), span(group)], r0.at[:, span(group)],
            send_sem.at[4], z_sem.at[0, group], half_peer(0),
        ).start()

    def stage_0(group):
        landed(r0.at[:, span(group)], z_sem.at[0, group])
        kept = z0[pl.ds(4 * bits[0], 4), span(group)].astype(F32)
        z1[:, span(group)] = (kept + r0[:, span(group)].astype(F32)).astype(BF16)
        remote(
            z1.at[pl.ds(2 - 2 * bits[1], 2), span(group)], r1.at[:, span(group)],
            send_sem.at[5], z_sem.at[1, group], half_peer(1),
        ).start()

    def stage_1(group):
        landed(r1.at[:, span(group)], z_sem.at[1, group])
        kept = z1[pl.ds(2 * bits[1], 2), span(group)].astype(F32)
        z2[:, span(group)] = (kept + r1[:, span(group)].astype(F32)).astype(BF16)
        remote(
            z2.at[1 - bits[2], span(group)], r2.at[span(group)],
            send_sem.at[6], z_sem.at[2, group], half_peer(2),
        ).start()

    def stage_2(group):
        landed(r2.at[span(group)], z_sem.at[2, group])

        @pl.loop(group * GROUP, group * GROUP + GROUP)
        def _(unit):
            total = z2[bits[2], unit].astype(F32) + r2[unit].astype(F32)
            total = total.astype(BF16)
            mine = jnp.where(c == 0, total[:, :8], total[:, 8:])
            other = jnp.where(c == 0, total[:, 8:], total[:, :8])
            slot, owners, j = place(unit)
            for k in range(2):
                wgrad_ref[:, pl.ds(column(owners[k], c, j), LANES)] = mine[k]
            wsend[unit] = other.reshape(ROWS, LANES)

    def swap(which, first, count):
        rows = pl.ds(first, count)
        remote(
            wsend.at[rows], wrecv.at[rows], send_sem.at[13], out_sem.at[which], core_peer
        ).start()

    def arrive_swap(which, first, count):
        rows = pl.ds(first, count)
        landed(wrecv.at[rows], out_sem.at[which])

        @pl.loop(first, first + count)
        def _(unit):
            slot, owners, j = place(unit)
            for k in range(2):
                wgrad_ref[:, pl.ds(column(owners[k], 1 - c, j), LANES)] = wrecv[
                    unit, k * 8:(k + 1) * 8
                ]

    def when(condition, work, *args):
        @pl.when(condition)
        def _():
            work(*args)

    EARLY = [
        (0, arrive_near, 0), (0, arrive_near, 1), (0, pass_on, 0), (0, arrive_near, 2),
        (0, arrive_weights), (1, pass_on, 1),
    ]
    LATE = [
        (2, arrive_far, 0), (2, pass_on, 2), (2, stage_mid, 0), (2, stage_mid, 1), (2, stage_mid, 2),
        (2, arrive_near, 3), (2, arrive_far, 1), (2, stage_y, 0), (2, stage_y, 1),
        (3, arrive_far, 2), (3, arrive_near, 4), (3, stage_y, 2), (3, stage_0, 0),
        (4, arrive_near, 5), (4, stage_0, 1), (4, stage_0, 2), (4, stage_mid, 3), (4, stage_1, 0),
        (4, stage_mid, 4),
    ]

    @pl.loop(0, GROUPS)
    def _(group):
        for at, work, *args in EARLY:
            when(group == at, work, *args)

        @pl.loop(group * GROUP, group * GROUP + GROUP)
        def _(unit):
            when(lax.rem(unit, GROUP) == 1, arrive_opposite, group)
            project(unit)

        for at, work, *args in LATE:
            when(group == at, work, *args)

    gains = [[None, None], [None, None]]

    def backward(image, head):
        pair = image * 2 + head
        rows = pl.ds(image * PATCHES, PATCHES)
        cols = pl.ds(head * HEAD, HEAD)
        grad = (acc[c, rows, cols] + accr[rows, cols]).astype(BF16)
        weights = probs[pair]
        vgrad_ref[rows, cols] = dot(weights.astype(BF16), grad).astype(BF16)
        upstream = dot(v[rows, cols], grad, NT)
        row_dot = jnp.sum(weights * upstream, axis=0, keepdims=True)
        score = (weights * (upstream - row_dot) * factor).astype(BF16)
        kup = dot(score, qu[pair])
        qup = dot(score, ku[pair], TN)
        for which, (up, normed, inverse, gain, out) in enumerate((
            (qup, qn[pair], qinv[pair], qg_ref[pl.ds(head, 1), :], qgrad_ref),
            (kup, kn[pair], kinv[pair], kg_ref[pl.ds(head, 1), :], kgrad_ref),
        )):
            term = jnp.sum(up * normed, axis=0, keepdims=True)
            old = gains[which][head]
            gains[which][head] = term if old is None else old + term
            out[rows, cols] = norm_backward(up, normed, inverse, gain).astype(BF16)

    for image in range(2):
        remote(
            acc.at[1 - c, part(image)], accr.at[part(image)],
            send_sem.at[12], acc_sem.at[image], core_peer,
        ).start()
    stage_y(3)
    stage_1(1)
    stage_1(2)
    stage_mid(5)
    for image in range(2):
        landed(accr.at[part(image)], acc_sem.at[image])
        for head in range(2):
            backward(image, head)

    gown[...] = jnp.zeros_like(gown)
    for which in range(2):
        for head in range(2):
            gown[pl.ds(which * 2 + head, 1), :] = gains[which][head] * (1.0 / 32.0)
    for k in (1, 3, 2):
        remote(gown, gy.at[k - 1], send_sem.at[7], gy_sem, y_peer(k)).start()

    def gain_pair(stage):
        remote(
            gsum.at[stage], gz.at[stage], send_sem.at[8 + stage], gz_sem.at[stage],
            half_peer(stage),
        ).start()

    stage_y(4)
    stage_y(5)
    stage_0(3)
    stage_0(4)
    for group in range(3):
        stage_2(group)
    landed(gy, gy_sem)
    gsum[0] = gown[...] + gy[0] + gy[1] + gy[2]
    gain_pair(0)
    stage_0(5)
    stage_1(3)
    stage_1(4)
    landed(gz.at[0], gz_sem.at[0])
    gsum[1] = gsum[0] + gz[0]
    gain_pair(1)
    stage_1(5)
    landed(gz.at[1], gz_sem.at[1])
    gsum[2] = gsum[1] + gz[1]
    gain_pair(2)
    stage_2(3)
    stage_2(4)
    swap(0, 0, 5 * GROUP)
    stage_2(5)
    swap(1, 5 * GROUP, GROUP)
    arrive_swap(0, 0, 5 * GROUP)
    landed(gz.at[2], gz_sem.at[2])
    total = gsum[2] + gz[2]
    qgg_ref[...] = total[0:2]
    kgg_ref[...] = total[2:4]

    arrive_swap(1, 5 * GROUP, GROUP)

    landed(ag.at[pl.ds(0, 2)], send_sem.at[0])
    landed(ag.at[pl.ds(0, 6)], send_sem.at[1])
    landed(w2.at[0], send_sem.at[2])
    landed(att.at[0], send_sem.at[11])
    landed(accr, send_sem.at[12])
    landed(wrecv, send_sem.at[13])
    landed(yrecv, send_sem.at[3])
    landed(r0, send_sem.at[4])
    landed(r1, send_sem.at[5])
    landed(r2, send_sem.at[6])
    landed(gy, send_sem.at[7])
    for stage in range(3):
        landed(gz.at[stage], send_sem.at[8 + stage])


def place_outputs(*refs):
    for source, target in zip(refs[:6], refs[6:]):
        target[...] = source[...]


def local(cotangent, out_weight, query_raw, key_raw, value, query_gain, key_gain):
    anywhere = pl.BlockSpec(memory_space=pl.ANY)
    vmem = pl.BlockSpec(memory_space=pltpu.VMEM)
    pair = (4, PATCHES, HEAD)
    outs = pl.pallas_call(
        kernel,
        out_shape=(
            jax.ShapeDtypeStruct((TOK, 256), BF16),
            jax.ShapeDtypeStruct((TOK, 256), BF16),
            jax.ShapeDtypeStruct((TOK, 256), BF16),
            jax.ShapeDtypeStruct((8, 6144), BF16),
            jax.ShapeDtypeStruct((2, HEAD), F32),
            jax.ShapeDtypeStruct((2, HEAD), F32),
        ),
        in_specs=[anywhere] * 5 + [vmem] * 2,
        out_specs=[vmem] * 6,
        scratch_shapes=[
            pltpu.VMEM((CHIPS, BLOCKS, TOK, LANES), BF16),
            pltpu.VMEM((BLOCKS, 2, 256, LANES), BF16),
            pltpu.VMEM((2, CHIPS, 256, 384), BF16),
            pltpu.VMEM((TOK, 256), BF16),
            pltpu.VMEM((TOK, 256), BF16),
            pltpu.VMEM((TOK, 256), BF16),
            pltpu.VMEM(pair, F32),
            pltpu.VMEM(pair, F32),
            pltpu.VMEM((4, PATCHES, 1), F32),
            pltpu.VMEM((4, PATCHES, 1), F32),
            pltpu.VMEM(pair, BF16),
            pltpu.VMEM(pair, BF16),
            pltpu.VMEM((4, PATCHES, PATCHES), F32),
            pltpu.VMEM((2, 256, TOK), BF16),
            pltpu.VMEM((2, TOK, 256), F32),
            pltpu.VMEM((TOK, 256), F32),
            pltpu.VMEM((UNITS, NY, NZ, 2, ROWS, LANES), BF16),
            pltpu.VMEM((UNITS, NY - 1, NZ, 2, ROWS, LANES), BF16),
            pltpu.VMEM((NZ, UNITS, 2, ROWS, LANES), BF16),
            pltpu.VMEM((4, UNITS, 2, ROWS, LANES), BF16),
            pltpu.VMEM((4, UNITS, 2, ROWS, LANES), BF16),
            pltpu.VMEM((2, UNITS, 2, ROWS, LANES), BF16),
            pltpu.VMEM((2, UNITS, 2, ROWS, LANES), BF16),
            pltpu.VMEM((UNITS, 2, ROWS, LANES), BF16),
            pltpu.VMEM((UNITS, ROWS, LANES), BF16),
            pltpu.VMEM((UNITS, ROWS, LANES), BF16),
            pltpu.VMEM((8, LANES), F32),
            pltpu.VMEM((NY - 1, 8, LANES), F32),
            pltpu.VMEM((3, 8, LANES), F32),
            pltpu.VMEM((3, 8, LANES), F32),
            pltpu.SemaphoreType.DMA((4 + BLOCKS,)),
            pltpu.SemaphoreType.DMA((14,)),
            pltpu.SemaphoreType.DMA((BLOCKS, 2)),
            pltpu.SemaphoreType.DMA((BLOCKS, 2)),
            pltpu.SemaphoreType.DMA((CHIPS, BLOCKS)),
            pltpu.SemaphoreType.DMA((2,)),
            pltpu.SemaphoreType.DMA((2,)),
            pltpu.SemaphoreType.DMA((2,)),
            pltpu.SemaphoreType.DMA((UNITS,)),
            pltpu.SemaphoreType.DMA((UNITS,)),
            pltpu.SemaphoreType.DMA((3, GROUPS)),
            pltpu.SemaphoreType.DMA,
            pltpu.SemaphoreType.DMA((3,)),
        ],
        compiler_params=pltpu.CompilerParams(
            collective_id=0, has_side_effects=True, vmem_limit_bytes=60 << 20
        ),
        cost_estimate=pl.CostEstimate(
            flops=4 * 10**9, bytes_accessed=6 * 10**6, transcendentals=4 * 65536
        ),
        name="attention_backward",
    )(cotangent, out_weight, query_raw, key_raw, value, query_gain, key_gain)
    return pl.pallas_call(
        place_outputs,
        out_shape=tuple(jax.ShapeDtypeStruct(out.shape, out.dtype) for out in outs),
        in_specs=[vmem] * 6,
        out_specs=[vmem] * 6,
        compiler_params=pltpu.CompilerParams(vmem_limit_bytes=60 << 20),
        name="place_outputs",
    )(*outs)


def solution(mesh):
    return jax.shard_map(
        local,
        mesh=mesh,
        in_specs=(
            P("dp", "mp"),
            P("mp", None),
            P("dp", "mp"),
            P("dp", "mp"),
            P("dp", "mp"),
            P("mp", None),
            P("mp", None),
        ),
        out_specs=(
            P("dp", "mp"),
            P("dp", "mp"),
            P("dp", "mp"),
            P(("mp", "dp"), None),
            P("mp", None),
            P("mp", None),
        ),
        check_vma=False,
    )
```

time: 101 us -> 92 us (0.911); the launches traced: 99.4 us -> 91.8 us
  local copies, waits for them, and re-layouts: 11 us -> 0 us
  Pallas kernels: 87.8 us -> 91.2 us
    unnamed x20 -> x0, local copies, waits for them, and re-layouts: 11 us -> none
    pallas_call x0 -> x1, Pallas kernels: none -> 2.09 us  [local(): pl.pallas_call(place_outputs, out_shape=tuple((jax.ShapeDtypeStruct(out.s...]
    pallas_call x1, Pallas kernels: 87.8 us -> 89.1 us  [local(): pl.pallas_call(kernel, out_shape=(jax.ShapeDtypeStruct((TOK, 256), BF16),...]
where the time goes in v2:
time: 92 us; the launch traced here: 91.8 us
  Pallas kernels  91.2 us (99%)
    pallas_call x1, Pallas kernels, local(): pl.pallas_call(kernel, out_shape=(jax.ShapeDtypeStruct((TOK, 256), BF16),...  89.1 us
    pallas_call x1, Pallas kernels, local(): pl.pallas_call(place_outputs, out_shape=tuple((jax.ShapeDtypeStruct(out.s...  2.09 us

profile of v2, /device:TPU:1, one launch (start us, length us, event | category | flops | bytes accessed | tf_op | source)
XLA Modules:
  0.0 91.8 jit_solution(8124666563068564629)
XLA Ops:
  0.6 89.1 %attention_backward.1 = (bf16[512,256]{1,0:T(8,128)(2,1)}, bf16[512,256]{1,0:T(8,128)(2,1)}, bf16[512,256]{1,0:T(8,128)(2,1)}, bf16[8,6144]{1,0:T(8,128)(2,1)}, f32[2,128]{1,0:T(2,128)}, /*index=5*/f32[2,128]{1,0:T(2,128)}) custom-call(bf16[512,384]{1,0:T(8,128)(2,1)} %cot_hbm.1, bf16[256,6144]{1,0:T(8,128)(2,1)} %w_hbm.1, bf16[512,256]{1,0:T(8,128)(2,1)} %q_hbm.1, ...), custom_call_target="tpu_custom_call" | custom-call | flops 4000000000 | bytes 6000000 | tf_op jit(solution)/shard_map/attention_backward/pallas_call | solution.py:474
  89.7 2.1 %place_outputs.1 = (bf16[512,256]{1,0:T(8,128)(2,1)}, bf16[512,256]{1,0:T(8,128)(2,1)}, bf16[512,256]{1,0:T(8,128)(2,1)}, bf16[8,6144]{1,0:T(8,128)(2,1)}, f32[2,128]{1,0:T(2,128)}, /*index=5*/f32[2,128]{1,0:T(2,128)}) custom-call(bf16[512,256]{1,0:T(8,128)(2,1)} %get-tuple-element.12.refs_0_, bf16[512,256]{1,0:T(8,128)(2,1)} %get-tuple-element.13.refs_1_, ...), custom_call_target="tpu_custom_call" | custom-call | tf_op jit(solution)/shard_map/place_outputs/pallas_call | solution.py:539

commit v3 on v2

--- a/solution.py
+++ b/solution.py
@@ -49,8 +49,8 @@
     cot_hbm, w_hbm, q_hbm, k_hbm, v_hbm, qg_ref, kg_ref,
     qgrad_ref, kgrad_ref, vgrad_ref, wgrad_ref, qgg_ref, kgg_ref,
     ag, transit, w2, qraw, kraw, v, qn, kn, qinv, kinv, qu, ku, probs, att, acc, accr,
-    ysend, yrecv, z0, r0, z1, r1, z2, r2, wsend, wrecv, gown, gy, gsum, gz,
-    local_sem, send_sem, leg_sem, far_sem, x_sem, core_sem, acc_sem, out_sem, y1_sem, y_sem, z_sem, gy_sem, gz_sem,
+    ysend, yrecv, z0, r0, z2, r2, gown, gy, gsum, gz,
+    local_sem, send_sem, leg_sem, far_sem, x_sem, core_sem, acc_sem, y1_sem, y_sem, z_sem, gy_sem, gz_sem,
 ):
     d = lax.axis_index("dp")
     m = lax.axis_index("mp")
@@ -72,14 +72,22 @@
         other = lax.rem(z + k, 2 * NZ)
         return (lax.rem(other, NZ) * NY + y, x * 4 + (other // NZ) * 2 + c)
 
-    def half_peer(stage):
+    def flip(stage):
         step = 1 << stage
-        return ((zl + step - 2 * step * bits[stage]) * NY + y, m)
+        return step - 2 * step * bits[stage]
+
+    def quad_peer(k):
+        return ((zl + flip(0) * (k // 2) + flip(1) * (k % 2)) * NY + y, m)
+
+    half_peer = ((zl + flip(2)) * NY + y, m)
+    half_cross = ((zl + flip(2)) * NY + y, m + 1 - 2 * c)
+    quad = bits[0] * 2 + bits[1]
 
     core_peer = (d, m + 1 - 2 * c)
 
     barrier = pltpu.get_barrier_semaphore()
-    peers = [z_peer(4), z_peer(12), core_peer, half_peer(0), half_peer(1)]
+    peers = [z_peer(4), z_peer(12), core_peer, half_cross]
+    peers += [quad_peer(k) for k in (1, 2, 3)]
     peers += [x_peer(k) for k in (1, 3)]
     peers += [y_peer(k) for k in (1, 2, 3)]
     for peer in peers:
@@ -148,22 +156,18 @@
         attended = dot(v[rows, cols], weights.astype(BF16), TN)
         att[c, cols, rows] = attended.astype(BF16)
 
-    for load in loads[:3]:
-        load.wait()
-    forward(0, 0)
-    forward(0, 1)
-    for load in loads[3:3 + BLOCKS]:
-        load.wait()
     pl.semaphore_wait(barrier, len(peers))
     def send_leg(j):
         for p in range(2):
             remote(
-                ag.at[0, j, part(p)], transit.at[j, p],
+                cot_hbm.at[part(p), pl.ds(j * LANES, LANES)], transit.at[j, p],
                 send_sem.at[0], leg_sem.at[j, p], z_peer(4 + 8 * p),
             ).start()
 
     send_leg(0)
     send_leg(1)
+    for load in loads[3:3 + BLOCKS]:
+        load.wait()
     for j in range(BLOCKS):
         send_x(0, j)
     for chip in range(CHIPS):
@@ -172,8 +176,11 @@
             w_hbm.at[:, pl.ds(start, 384)], w2.at[c, chip],
             send_sem.at[2], core_sem.at[0], core_peer,
         ).start()
-    forward(1, 0)
-    forward(1, 1)
+    for load in loads[:3]:
+        load.wait()
+    for image in range(2):
+        for head in range(2):
+            forward(image, head)
     remote(att.at[c], att.at[c], send_sem.at[11], core_sem.at[1], core_peer).start()
     acc[...] = jnp.zeros_like(acc)
     landed(w2.at[c], local_sem.at[3 + BLOCKS])
@@ -239,15 +246,12 @@
         slot, owners, j = place(unit)
         cols = pl.ds(pl.multiple_of(j * LANES, LANES), LANES)
         block = jnp.concatenate([ag[slot, j], ag[slot + 2, j]], axis=1)
-        terms = [
-            (dot(att[core], block) * (1.0 / 32.0)).reshape(NZ, NY, 8, 2 * LANES)
-            for core in range(2)
-        ]
-        both = jnp.concatenate(terms, axis=2).astype(BF16)
-        for to in range(NZ):
-            for p in range(NY):
-                for k in range(2):
-                    ysend[unit, p, REVERSED[to], k] = both[to, p, :, k * LANES:(k + 1) * LANES]
+        for core in range(2):
+            terms = (dot(att[core], block) * (1.0 / 32.0)).reshape(NZ, NY, 8, 2 * LANES)
+            both = jnp.concatenate([terms[..., :LANES], terms[..., LANES:]], axis=2).astype(BF16)
+            for to in range(NZ):
+                for p in range(NY):
+                    ysend[unit, p, REVERSED[to], core] = both[to, p]
         send_y(unit, across, 0, 0, y1_sem, 1)
         send_y(unit, across, 1, 0, y1_sem, 3)
         send_y(unit, up, 1, 1, y_sem, 1)
@@ -280,60 +284,40 @@
                 total += yrecv[unit, k].astype(F32)
             z0[:, unit] = total.astype(BF16)
 
-        remote(
-            z0.at[pl.ds(4 - 4 * bits[0], 4), span(group)], r0.at[:, span(group)],
-            send_sem.at[4], z_sem.at[0, group], half_peer(0),
-        ).start()
+        for k in (1, 2, 3):
+            other = lax.rem(bits[0] + k // 2, 2) * 2 + lax.rem(bits[1] + k % 2, 2)
+            remote(
+                z0.at[pl.ds(2 * other, 2), span(group)], r0.at[k - 1, :, span(group)],
+                send_sem.at[4], z_sem.at[0, group], quad_peer(k),
+            ).start()
 
     def stage_0(group):
-        landed(r0.at[:, span(group)], z_sem.at[0, group])
-        kept = z0[pl.ds(4 * bits[0], 4), span(group)].astype(F32)
-        z1[:, span(group)] = (kept + r0[:, span(group)].astype(F32)).astype(BF16)
-        remote(
-            z1.at[pl.ds(2 - 2 * bits[1], 2), span(group)], r1.at[:, span(group)],
-            send_sem.at[5], z_sem.at[1, group], half_peer(1),
-        ).start()
-
-    def stage_1(group):
-        landed(r1.at[:, span(group)], z_sem.at[1, group])
-        kept = z1[pl.ds(2 * bits[1], 2), span(group)].astype(F32)
-        z2[:, span(group)] = (kept + r1[:, span(group)].astype(F32)).astype(BF16)
-        remote(
-            z2.at[1 - bits[2], span(group)], r2.at[span(group)],
-            send_sem.at[6], z_sem.at[2, group], half_peer(2),
-        ).start()
+        landed(r0.at[:, :, span(group)], z_sem.at[0, group])
+        total = z0[pl.ds(2 * quad, 2), span(group)].astype(F32)
+        for k in range(3):
+            total += r0[k, :, span(group)].astype(F32)
+        z2[:, span(group)] = total.astype(BF16)
+        for source, slot, peer in (
+            (z2.at[1 - bits[2], span(group), c], 0, half_peer),
+            (z2.at[1 - bits[2], span(group), 1 - c], 1, half_cross),
+            (z2.at[bits[2], span(group), 1 - c], 2, core_peer),
+        ):
+            remote(
+                source, r2.at[slot, span(group)], send_sem.at[5], z_sem.at[1, group], peer
+            ).start()
 
     def stage_2(group):
-        landed(r2.at[span(group)], z_sem.at[2, group])
+        landed(r2.at[:, span(group)], z_sem.at[1, group])
 
         @pl.loop(group * GROUP, group * GROUP + GROUP)
         def _(unit):
-            total = z2[bits[2], unit].astype(F32) + r2[unit].astype(F32)
-            total = total.astype(BF16)
-            mine = jnp.where(c == 0, total[:, :8], total[:, 8:])
-            other = jnp.where(c == 0, total[:, 8:], total[:, :8])
             slot, owners, j = place(unit)
+            mine = (z2[bits[2], unit, c].astype(F32) + r2[0, unit].astype(F32)).astype(BF16)
+            other = (r2[1, unit].astype(F32) + r2[2, unit].astype(F32)).astype(BF16)
             for k in range(2):
-                wgrad_ref[:, pl.ds(column(owners[k], c, j), LANES)] = mine[k]
-            wsend[unit] = other.reshape(ROWS, LANES)
-
-    def swap(which, first, count):
-        rows = pl.ds(first, count)
-        remote(
-            wsend.at[rows], wrecv.at[rows], send_sem.at[13], out_sem.at[which], core_peer
-        ).start()
-
-    def arrive_swap(which, first, count):
-        rows = pl.ds(first, count)
-        landed(wrecv.at[rows], out_sem.at[which])
-
-        @pl.loop(first, first + count)
-        def _(unit):
-            slot, owners, j = place(unit)
-            for k in range(2):
-                wgrad_ref[:, pl.ds(column(owners[k], 1 - c, j), LANES)] = wrecv[
-                    unit, k * 8:(k + 1) * 8
-                ]
+                rows = slice(k * 8, k * 8 + 8)
+                wgrad_ref[:, pl.ds(column(owners[k], c, j), LANES)] = mine[rows]
+                wgrad_ref[:, pl.ds(column(owners[k], 1 - c, j), LANES)] = other[rows]
 
     def when(condition, work, *args):
         @pl.when(condition)
@@ -347,9 +331,8 @@
     LATE = [
         (2, arrive_far, 0), (2, pass_on, 2), (2, stage_mid, 0), (2, stage_mid, 1), (2, stage_mid, 2),
         (2, arrive_near, 3), (2, arrive_far, 1), (2, stage_y, 0), (2, stage_y, 1),
-        (3, arrive_far, 2), (3, arrive_near, 4), (3, stage_y, 2), (3, stage_0, 0),
-        (4, arrive_near, 5), (4, stage_0, 1), (4, stage_0, 2), (4, stage_mid, 3), (4, stage_1, 0),
-        (4, stage_mid, 4),
+        (3, arrive_far, 2), (3, arrive_near, 4), (3, stage_y, 2),
+        (4, stage_mid, 3), (4, arrive_near, 5), (4, stage_0, 0), (4, stage_0, 1), (4, stage_0, 2),
     ]
 
     @pl.loop(0, GROUPS)
@@ -359,6 +342,7 @@
 
         @pl.loop(group * GROUP, group * GROUP + GROUP)
         def _(unit):
+            when(unit == UNITS - 1, stage_mid, GROUPS - 2)
             when(lax.rem(unit, GROUP) == 1, arrive_opposite, group)
             project(unit)
 
@@ -394,8 +378,7 @@
             send_sem.at[12], acc_sem.at[image], core_peer,
         ).start()
     stage_y(3)
-    stage_1(1)
-    stage_1(2)
+    stage_2(0)
     stage_mid(5)
     for image in range(2):
         landed(accr.at[part(image)], acc_sem.at[image])
@@ -409,57 +392,41 @@
     for k in (1, 3, 2):
         remote(gown, gy.at[k - 1], send_sem.at[7], gy_sem, y_peer(k)).start()
 
-    def gain_pair(stage):
-        remote(
-            gsum.at[stage], gz.at[stage], send_sem.at[8 + stage], gz_sem.at[stage],
-            half_peer(stage),
-        ).start()
-
     stage_y(4)
     stage_y(5)
     stage_0(3)
-    stage_0(4)
-    for group in range(3):
-        stage_2(group)
     landed(gy, gy_sem)
     gsum[0] = gown[...] + gy[0] + gy[1] + gy[2]
-    gain_pair(0)
+    for k in (1, 2, 3):
+        remote(
+            gsum.at[0], gz.at[k - 1], send_sem.at[6], gz_sem.at[0], quad_peer(k)
+        ).start()
+    stage_0(4)
+    stage_2(1)
+    stage_2(2)
     stage_0(5)
-    stage_1(3)
-    stage_1(4)
-    landed(gz.at[0], gz_sem.at[0])
-    gsum[1] = gsum[0] + gz[0]
-    gain_pair(1)
-    stage_1(5)
-    landed(gz.at[1], gz_sem.at[1])
-    gsum[2] = gsum[1] + gz[1]
-    gain_pair(2)
+    landed(gz.at[pl.ds(0, 3)], gz_sem.at[0])
+    gsum[1] = gsum[0] + gz[0] + gz[1] + gz[2]
+    remote(gsum.at[1], gz.at[3], send_sem.at[8], gz_sem.at[1], half_peer).start()
     stage_2(3)
     stage_2(4)
-    swap(0, 0, 5 * GROUP)
     stage_2(5)
-    swap(1, 5 * GROUP, GROUP)
-    arrive_swap(0, 0, 5 * GROUP)
-    landed(gz.at[2], gz_sem.at[2])
-    total = gsum[2] + gz[2]
+    landed(gz.at[3], gz_sem.at[1])
+    total = gsum[1] + gz[3]
     qgg_ref[...] = total[0:2]
     kgg_ref[...] = total[2:4]
-
-    arrive_swap(1, 5 * GROUP, GROUP)
 
     landed(ag.at[pl.ds(0, 2)], send_sem.at[0])
     landed(ag.at[pl.ds(0, 6)], send_sem.at[1])
     landed(w2.at[0], send_sem.at[2])
     landed(att.at[0], send_sem.at[11])
     landed(accr, send_sem.at[12])
-    landed(wrecv, send_sem.at[13])
     landed(yrecv, send_sem.at[3])
     landed(r0, send_sem.at[4])
-    landed(r1, send_sem.at[5])
-    landed(r2, send_sem.at[6])
+    landed(r2, send_sem.at[5])
+    landed(gz.at[pl.ds(0, 3)], send_sem.at[6])
     landed(gy, send_sem.at[7])
-    for stage in range(3):
-        landed(gz.at[stage], send_sem.at[8 + stage])
+    landed(gz.at[3], send_sem.at[8])
 
 
 def place_outputs(*refs):
@@ -503,30 +470,25 @@
             pltpu.VMEM((UNITS, NY, NZ, 2, ROWS, LANES), BF16),
             pltpu.VMEM((UNITS, NY - 1, NZ, 2, ROWS, LANES), BF16),
             pltpu.VMEM((NZ, UNITS, 2, ROWS, LANES), BF16),
-            pltpu.VMEM((4, UNITS, 2, ROWS, LANES), BF16),
-            pltpu.VMEM((4, UNITS, 2, ROWS, LANES), BF16),
+            pltpu.VMEM((3, 2, UNITS, 2, ROWS, LANES), BF16),
             pltpu.VMEM((2, UNITS, 2, ROWS, LANES), BF16),
-            pltpu.VMEM((2, UNITS, 2, ROWS, LANES), BF16),
-            pltpu.VMEM((UNITS, 2, ROWS, LANES), BF16),
-            pltpu.VMEM((UNITS, ROWS, LANES), BF16),
-            pltpu.VMEM((UNITS, ROWS, LANES), BF16),
+            pltpu.VMEM((3, UNITS, ROWS, LANES), BF16),
             pltpu.VMEM((8, LANES), F32),
             pltpu.VMEM((NY - 1, 8, LANES), F32),
-            pltpu.VMEM((3, 8, LANES), F32),
-            pltpu.VMEM((3, 8, LANES), F32),
+            pltpu.VMEM((2, 8, LANES), F32),
+            pltpu.VMEM((4, 8, LANES), F32),
             pltpu.SemaphoreType.DMA((4 + BLOCKS,)),
-            pltpu.SemaphoreType.DMA((14,)),
+            pltpu.SemaphoreType.DMA((13,)),
             pltpu.SemaphoreType.DMA((BLOCKS, 2)),
             pltpu.SemaphoreType.DMA((BLOCKS, 2)),
             pltpu.SemaphoreType.DMA((CHIPS, BLOCKS)),
             pltpu.SemaphoreType.DMA((2,)),
             pltpu.SemaphoreType.DMA((2,)),
-            pltpu.SemaphoreType.DMA((2,)),
             pltpu.SemaphoreType.DMA((UNITS,)),
             pltpu.SemaphoreType.DMA((UNITS,)),
-            pltpu.SemaphoreType.DMA((3, GROUPS)),
+            pltpu.SemaphoreType.DMA((2, GROUPS)),
             pltpu.SemaphoreType.DMA,
-            pltpu.SemaphoreType.DMA((3,)),
+            pltpu.SemaphoreType.DMA((2,)),
         ],
         compiler_params=pltpu.CompilerParams(
             collective_id=0, has_side_effects=True, vmem_limit_bytes=60 << 20

time: 92 us -> 88.9 us (0.966)
  Pallas kernels: 91.2 us -> 88.1 us
    pallas_call x1, Pallas kernels: 89.1 us -> 86 us  [local(): pl.pallas_call(kernel, out_shape=(jax.ShapeDtypeStruct((TOK, 256), BF16),...]
where the time goes in v3:
time: 88.9 us; the launch traced here: 88.7 us
  Pallas kernels  88.1 us (99%)
    pallas_call x1, Pallas kernels, local(): pl.pallas_call(kernel, out_shape=(jax.ShapeDtypeStruct((TOK, 256), BF16),...  86 us
    pallas_call x1, Pallas kernels, local(): pl.pallas_call(place_outputs, out_shape=tuple((jax.ShapeDtypeStruct(out.s...  2.09 us

profile of v3, /device:TPU:1, one launch (start us, length us, event | category | flops | bytes accessed | tf_op | source)
XLA Modules:
  0.0 88.7 jit_solution(7872082859541880952)
XLA Ops:
  0.6 86.0 %attention_backward.1 = (bf16[512,256]{1,0:T(8,128)(2,1)}, bf16[512,256]{1,0:T(8,128)(2,1)}, bf16[512,256]{1,0:T(8,128)(2,1)}, bf16[8,6144]{1,0:T(8,128)(2,1)}, f32[2,128]{1,0:T(2,128)}, /*index=5*/f32[2,128]{1,0:T(2,128)}) custom-call(bf16[512,384]{1,0:T(8,128)(2,1)} %cot_hbm.1, bf16[256,6144]{1,0:T(8,128)(2,1)} %w_hbm.1, bf16[512,256]{1,0:T(8,128)(2,1)} %q_hbm.1, ...), custom_call_target="tpu_custom_call" | custom-call | flops 4000000000 | bytes 6000000 | tf_op jit(solution)/shard_map/attention_backward/pallas_call | solution.py:441
  86.6 2.1 %place_outputs.1 = (bf16[512,256]{1,0:T(8,128)(2,1)}, bf16[512,256]{1,0:T(8,128)(2,1)}, bf16[512,256]{1,0:T(8,128)(2,1)}, bf16[8,6144]{1,0:T(8,128)(2,1)}, f32[2,128]{1,0:T(2,128)}, /*index=5*/f32[2,128]{1,0:T(2,128)}) custom-call(bf16[512,256]{1,0:T(8,128)(2,1)} %get-tuple-element.12.refs_0_, bf16[512,256]{1,0:T(8,128)(2,1)} %get-tuple-element.13.refs_1_, ...), custom_call_target="tpu_custom_call" | custom-call | tf_op jit(solution)/shard_map/place_outputs/pallas_call | solution.py:501

commit v4 on v3

--- a/solution.py
+++ b/solution.py
@@ -262,11 +262,8 @@
                 block = jnp.concatenate([ag[slot, j, part(p)], ag[slot + 2, j, part(p)]], axis=1)
                 acc[core, part(p), :] += dot(block, weight, NT)
 
-    def span(group):
-        return pl.ds(group * GROUP, GROUP)
-
-    def stage_mid(group):
-        @pl.loop(group * GROUP, group * GROUP + GROUP)
+    def stage_mid(first, count=GROUP):
+        @pl.loop(first, first + count)
         def _(unit):
             landed(yrecv.at[unit, 0], y1_sem.at[unit])
             for to, p, slot, k in ((up, 0, 1, 1), (down, 1, 2, 3)):
@@ -275,8 +272,10 @@
                 ysend[unit, to, quads(p)] = total.astype(BF16)
                 send_y(unit, to, p, slot, y_sem, k)
 
-    def stage_y(group):
-        @pl.loop(group * GROUP, group * GROUP + GROUP)
+    def stage_y(first, count=GROUP):
+        span = pl.ds(first, count)
+
+        @pl.loop(first, first + count)
         def _(unit):
             landed(yrecv.at[unit, pl.ds(1, 2)], y_sem.at[unit])
             total = ysend[unit, y].astype(F32)
@@ -287,29 +286,31 @@
         for k in (1, 2, 3):
             other = lax.rem(bits[0] + k // 2, 2) * 2 + lax.rem(bits[1] + k % 2, 2)
             remote(
-                z0.at[pl.ds(2 * other, 2), span(group)], r0.at[k - 1, :, span(group)],
-                send_sem.at[4], z_sem.at[0, group], quad_peer(k),
+                z0.at[pl.ds(2 * other, 2), span], r0.at[k - 1, :, span],
+                send_sem.at[4], z_sem.at[0, first], quad_peer(k),
             ).start()
 
-    def stage_0(group):
-        landed(r0.at[:, :, span(group)], z_sem.at[0, group])
-        total = z0[pl.ds(2 * quad, 2), span(group)].astype(F32)
+    def stage_0(first, count=GROUP):
+        span = pl.ds(first, count)
+        landed(r0.at[:, :, span], z_sem.at[0, first])
+        total = z0[pl.ds(2 * quad, 2), span].astype(F32)
         for k in range(3):
-            total += r0[k, :, span(group)].astype(F32)
-        z2[:, span(group)] = total.astype(BF16)
+            total += r0[k, :, span].astype(F32)
+        z2[:, span] = total.astype(BF16)
         for source, slot, peer in (
-            (z2.at[1 - bits[2], span(group), c], 0, half_peer),
-            (z2.at[1 - bits[2], span(group), 1 - c], 1, half_cross),
-            (z2.at[bits[2], span(group), 1 - c], 2, core_peer),
+            (z2.at[1 - bits[2], span, c], 0, half_peer),
+            (z2.at[1 - bits[2], span, 1 - c], 1, half_cross),
+            (z2.at[bits[2], span, 1 - c], 2, core_peer),
         ):
             remote(
-                source, r2.at[slot, span(group)], send_sem.at[5], z_sem.at[1, group], peer
+                source, r2.at[slot, span], send_sem.at[5], z_sem.at[1, first], peer
             ).start()
 
-    def stage_2(group):
-        landed(r2.at[:, span(group)], z_sem.at[1, group])
-
-        @pl.loop(group * GROUP, group * GROUP + GROUP)
+    def stage_2(first, count=GROUP):
+        span = pl.ds(first, count)
+        landed(r2.at[:, span], z_sem.at[1, first])
+
+        @pl.loop(first, first + count)
         def _(unit):
             slot, owners, j = place(unit)
             mine = (z2[bits[2], unit, c].astype(F32) + r2[0, unit].astype(F32)).astype(BF16)
@@ -329,10 +330,10 @@
         (0, arrive_weights), (1, pass_on, 1),
     ]
     LATE = [
-        (2, arrive_far, 0), (2, pass_on, 2), (2, stage_mid, 0), (2, stage_mid, 1), (2, stage_mid, 2),
-        (2, arrive_near, 3), (2, arrive_far, 1), (2, stage_y, 0), (2, stage_y, 1),
-        (3, arrive_far, 2), (3, arrive_near, 4), (3, stage_y, 2),
-        (4, stage_mid, 3), (4, arrive_near, 5), (4, stage_0, 0), (4, stage_0, 1), (4, stage_0, 2),
+        (2, arrive_far, 0), (2, pass_on, 2), (2, stage_mid, 0), (2, stage_mid, 2), (2, stage_mid, 4),
+        (2, arrive_near, 3), (2, arrive_far, 1), (2, stage_y, 0), (2, stage_y, 2),
+        (3, arrive_far, 2), (3, arrive_near, 4), (3, stage_y, 4),
+        (4, stage_mid, 6), (4, stage_0, 0), (4, stage_0, 2), (4, stage_0, 4),
     ]
 
     @pl.loop(0, GROUPS)
@@ -342,7 +343,8 @@
 
         @pl.loop(group * GROUP, group * GROUP + GROUP)
         def _(unit):
-            when(unit == UNITS - 1, stage_mid, GROUPS - 2)
+            when(unit == 9, arrive_near, 5)
+            when(unit == 11, stage_mid, 8)
             when(lax.rem(unit, GROUP) == 1, arrive_opposite, group)
             project(unit)
 
@@ -377,14 +379,17 @@
             acc.at[1 - c, part(image)], accr.at[part(image)],
             send_sem.at[12], acc_sem.at[image], core_peer,
         ).start()
-    stage_y(3)
-    stage_2(0)
-    stage_mid(5)
-    for image in range(2):
+
+    def backward_image(image):
         landed(accr.at[part(image)], acc_sem.at[image])
         for head in range(2):
             backward(image, head)
 
+    stage_y(6)
+    stage_mid(10, 1)
+    backward_image(0)
+    stage_mid(11, 1)
+    backward_image(1)
     gown[...] = jnp.zeros_like(gown)
     for which in range(2):
         for head in range(2):
@@ -392,25 +397,29 @@
     for k in (1, 3, 2):
         remote(gown, gy.at[k - 1], send_sem.at[7], gy_sem, y_peer(k)).start()
 
-    stage_y(4)
-    stage_y(5)
-    stage_0(3)
+    stage_y(8)
+    stage_y(10, 1)
+    stage_y(11, 1)
+    stage_2(0)
+    stage_0(6)
     landed(gy, gy_sem)
     gsum[0] = gown[...] + gy[0] + gy[1] + gy[2]
     for k in (1, 2, 3):
         remote(
             gsum.at[0], gz.at[k - 1], send_sem.at[6], gz_sem.at[0], quad_peer(k)
         ).start()
-    stage_0(4)
-    stage_2(1)
+    stage_0(8)
     stage_2(2)
-    stage_0(5)
+    stage_2(4)
+    stage_0(10, 1)
+    stage_0(11, 1)
     landed(gz.at[pl.ds(0, 3)], gz_sem.at[0])
     gsum[1] = gsum[0] + gz[0] + gz[1] + gz[2]
     remote(gsum.at[1], gz.at[3], send_sem.at[8], gz_sem.at[1], half_peer).start()
-    stage_2(3)
-    stage_2(4)
-    stage_2(5)
+    stage_2(6)
+    stage_2(8)
+    stage_2(10, 1)
+    stage_2(11, 1)
     landed(gz.at[3], gz_sem.at[1])
     total = gsum[1] + gz[3]
     qgg_ref[...] = total[0:2]
@@ -486,7 +495,7 @@
             pltpu.SemaphoreType.DMA((2,)),
             pltpu.SemaphoreType.DMA((UNITS,)),
             pltpu.SemaphoreType.DMA((UNITS,)),
-            pltpu.SemaphoreType.DMA((2, GROUPS)),
+            pltpu.SemaphoreType.DMA((2, UNITS)),
             pltpu.SemaphoreType.DMA,
             pltpu.SemaphoreType.DMA((2,)),
         ],

time: 88.9 us -> 87.9 us (0.989)
  Pallas kernels: 88.1 us -> 87.1 us
    pallas_call x1, Pallas kernels: 86 us -> 85 us  [local(): pl.pallas_call(kernel, out_shape=(jax.ShapeDtypeStruct((TOK, 256), BF16),...]
where the time goes in v4:
time: 87.9 us; the launch traced here: 87.7 us
  Pallas kernels  87.1 us (99%)
    pallas_call x1, Pallas kernels, local(): pl.pallas_call(kernel, out_shape=(jax.ShapeDtypeStruct((TOK, 256), BF16),...  85 us
    pallas_call x1, Pallas kernels, local(): pl.pallas_call(place_outputs, out_shape=tuple((jax.ShapeDtypeStruct(out.s...  2.09 us

profile of v4, /device:TPU:1, one launch (start us, length us, event | category | flops | bytes accessed | tf_op | source)
XLA Modules:
  0.0 87.7 jit_solution(1242353964883213285)
XLA Ops:
  0.6 85.0 %attention_backward.1 = (bf16[512,256]{1,0:T(8,128)(2,1)}, bf16[512,256]{1,0:T(8,128)(2,1)}, bf16[512,256]{1,0:T(8,128)(2,1)}, bf16[8,6144]{1,0:T(8,128)(2,1)}, f32[2,128]{1,0:T(2,128)}, /*index=5*/f32[2,128]{1,0:T(2,128)}) custom-call(bf16[512,384]{1,0:T(8,128)(2,1)} %cot_hbm.1, bf16[256,6144]{1,0:T(8,128)(2,1)} %w_hbm.1, bf16[512,256]{1,0:T(8,128)(2,1)} %q_hbm.1, ...), custom_call_target="tpu_custom_call" | custom-call | flops 4000000000 | bytes 6000000 | tf_op jit(solution)/shard_map/attention_backward/pallas_call | solution.py:450
  85.6 2.1 %place_outputs.1 = (bf16[512,256]{1,0:T(8,128)(2,1)}, bf16[512,256]{1,0:T(8,128)(2,1)}, bf16[512,256]{1,0:T(8,128)(2,1)}, bf16[8,6144]{1,0:T(8,128)(2,1)}, f32[2,128]{1,0:T(2,128)}, /*index=5*/f32[2,128]{1,0:T(2,128)}) custom-call(bf16[512,256]{1,0:T(8,128)(2,1)} %get-tuple-element.12.refs_0_, bf16[512,256]{1,0:T(8,128)(2,1)} %get-tuple-element.13.refs_1_, ...), custom_call_target="tpu_custom_call" | custom-call | tf_op jit(solution)/shard_map/place_outputs/pallas_call | solution.py:510
